TPU v7x, 32 devices: a whole 2x2x4 slice. The times are simulated.
32 devices in a mesh: row: 4 (over x, core), col: 8 (over z, y).
Axes of the slice: x: 2, y: 2, z: 4, core: 2. Of those that a mesh axis runs over, the one named last changes fastest.
Arguments:
- density: bfloat16 [1024, 3, 256], P(('row', 'col')), may hold values from -6 to 6
- coords: bfloat16 [1024, 3, 256], P(('row', 'col')), may hold values from 0 to 1
- basis: bfloat16 [1024, 32, 768], P(('row', 'col')), may hold values from -0.21875 to 0.21875
- transfer: float32 [1024, 32, 32], P(('row', 'col')), may hold values from -1 to 1
- parent: int32 [1024], replicated, may hold values from 0 to 255
- near_pairs: int32 [2, 4096], P(None, ('row', 'col')), may hold values from 0 to 1023, as said below
- near_count: int32 [32], P(('row', 'col')), may hold values from 16 to 128, as said below
- far_pairs: int32 [2, 2048], P(None, ('row', 'col')), may hold values from 0 to 255
- coupling: float32 [2048, 32, 32], P(('row', 'col')), may hold values from -1 to 1
Outputs:
- velocity: float32 [1024, 3, 256], P(('row', 'col'))
Inputs may be any that keep to these rules, and one draw needn't show every extreme that they name: `near_pairs`: let i = j % 128 for slot j of device (r, c), owners in row-major order with 32 clusters each. The first cluster is owned by device (r, i // (128 // 8)) and the second by device (i // (128 // 4), c); the two may be equal. Slots past a device's live count hold valid but unused pairs. `near_count`: the largest live count equals 128 in every draw.
All inputs are finite; a program needn't handle non-finite values.
Results may differ from a plain program's by a relative error of at most 0.0026.
Values may be sent and summed in bfloat16 or wider, within the bound.
A program may use at most 64 MiB of HBM per device.

v0:
```python
import functools
import math

import jax
import jax.numpy as jnp
from jax import lax
from jax.experimental import pallas as pl
from jax.experimental.pallas import tpu as pltpu
from jax.sharding import PartitionSpec as P

REG_EPS = 0.02
STOKES_SCALE = 1.0 / (8.0 * math.pi)
MESH = pl.DeviceIdType.MESH
GROUP = 4
CHUNK = 16


def greet(n_row, n_col, row, col):
    barrier = pltpu.get_barrier_semaphore()
    for k in range(1, n_col):
        pl.semaphore_signal(barrier, inc=1, device_id=(row, lax.rem(col + k, n_col)), device_id_type=MESH)
    for k in range(1, n_row):
        pl.semaphore_signal(barrier, inc=1, device_id=(lax.rem(row + k, n_row), col), device_id_type=MESH)
    pl.semaphore_wait(barrier, n_col + n_row - 2)


def part(ref, index, size):
    return ref.at[pl.ds(pl.multiple_of(index * size, size), size)]


def gather_kernel(n_row, n_col, n_z, tile, ids, lifted, row_tiles, col_tiles, row_ids, col_ids, all_lifted,
                  own_sem, st, rt, sct, rct, si, ri, sci, rci, sl, rl, scl, rcl):
    row, col = lax.axis_index("row"), lax.axis_index("col")
    n_y = n_col // n_z
    z, y = col // n_y, lax.rem(col, n_y)
    rows, lift_rows = tile.shape[0], lifted.shape[0]
    span = n_col * lift_rows
    own = [
        pltpu.make_async_copy(tile, part(row_tiles, col, rows), own_sem.at[0]),
        pltpu.make_async_copy(tile, part(col_tiles, row, rows), own_sem.at[1]),
        pltpu.make_async_copy(ids, row_ids.at[col], own_sem.at[2]),
        pltpu.make_async_copy(ids, col_ids.at[row], own_sem.at[3]),
        pltpu.make_async_copy(lifted, part(all_lifted, row * n_col + col, lift_rows), own_sem.at[4]),
    ]
    for copy in own:
        copy.start()
    greet(n_row, n_col, row, col)

    def to_col(src, dst, index, size, sends, recvs, slot, peer):
        return pltpu.make_async_remote_copy(
            src_ref=src, dst_ref=part(dst, index, size), send_sem=sends.at[slot], recv_sem=recvs.at[index],
            device_id=(row, peer), device_id_type=MESH)

    def to_row(src, dst_view, sends, recvs, peer):
        return pltpu.make_async_remote_copy(
            src_ref=src, dst_ref=dst_view, send_sem=sends.at[peer], recv_sem=recvs.at[row],
            device_id=(peer, col), device_id_type=MESH)

    started = []

    def go(copy):
        copy.start()
        started.append(copy)

    for k in range(1, n_col):
        peer = lax.rem(col + k, n_col)
        go(pltpu.make_async_remote_copy(
            src_ref=lifted, dst_ref=part(all_lifted, row * n_col + col, lift_rows),
            send_sem=sl.at[peer], recv_sem=rl.at[col], device_id=(row, peer), device_id_type=MESH))
    for k in range(1, n_z):
        peer = lax.rem(z + k, n_z) * n_y + y
        go(to_col(tile, row_tiles, col, rows, st, rt, k, peer))
    for k in range(1, n_y):
        peer = z * n_y + lax.rem(y + k, n_y)
        go(to_col(tile, row_tiles, col, rows, st, rt, n_z + k, peer))
    for k in range(1, n_row):
        peer = lax.rem(row + k, n_row)
        go(to_row(tile, part(col_tiles, row, rows), sct, rct, peer))
        go(to_row(ids, col_ids.at[row], sci, rci, peer))
    for k in range(1, n_col):
        peer = lax.rem(col + k, n_col)
        go(pltpu.make_async_remote_copy(
            src_ref=ids, dst_ref=row_ids.at[col], send_sem=si.at[peer], recv_sem=ri.at[col],
            device_id=(row, peer), device_id_type=MESH))

    own[4].wait()
    for k in range(1, n_col):
        src = lax.rem(col + k, n_col)
        pltpu.make_async_copy(lifted, part(all_lifted, row * n_col + src, lift_rows), rl.at[src]).wait()
    for k in range(1, n_row):
        peer = lax.rem(row + k, n_row)
        mine = part(all_lifted, row, span)
        go(to_row(mine, mine, scl, rcl, peer))

    for k in range(1, n_z):
        src = lax.rem(z + k, n_z) * n_y + y
        pltpu.make_async_copy(tile, part(row_tiles, src, rows), rt.at[src]).wait()
        for j in range(1, n_y):
            peer = z * n_y + lax.rem(y + j, n_y)
            go(to_col(part(row_tiles, src, rows), row_tiles, src, rows, st, rt, n_z + n_y * k + j, peer))
    for j in range(1, n_y):
        for k in range(n_z):
            src = lax.rem(z + k, n_z) * n_y + lax.rem(y + j, n_y)
            pltpu.make_async_copy(tile, part(row_tiles, src, rows), rt.at[src]).wait()
    for k in range(1, n_col):
        src = lax.rem(col + k, n_col)
        pltpu.make_async_copy(ids, row_ids.at[src], ri.at[src]).wait()
    for k in range(1, n_row):
        src = lax.rem(row + k, n_row)
        pltpu.make_async_copy(tile, part(col_tiles, src, rows), rct.at[src]).wait()
        pltpu.make_async_copy(ids, col_ids.at[src], rci.at[src]).wait()
        view = part(all_lifted, src, span)
        pltpu.make_async_copy(view, view, rcl.at[src]).wait()
    for copy in own[:4]:
        copy.wait()
    for copy in started:
        copy.wait_send()


def gather(n_row, n_col, tile, ids, lifted):
    n_z = 4 if n_col % 4 == 0 else 1
    any_space = pl.BlockSpec(memory_space=pl.ANY)
    dma = pltpu.SemaphoreType.DMA
    sizes = [(5,), (n_z * (n_col // n_z + 1) + n_col,), (n_col,), (n_row,), (n_row,), (n_col,), (n_col,),
             (n_row,), (n_row,), (n_col,), (n_col,), (n_row,), (n_row,)]
    shape = jax.ShapeDtypeStruct
    return pl.pallas_call(
        functools.partial(gather_kernel, n_row, n_col, n_z),
        out_shape=[
            shape((n_col * tile.shape[0], tile.shape[1]), tile.dtype),
            shape((n_row * tile.shape[0], tile.shape[1]), tile.dtype),
            shape((n_col,) + ids.shape, ids.dtype),
            shape((n_row,) + ids.shape, ids.dtype),
            shape((n_row * n_col * lifted.shape[0], lifted.shape[1]), lifted.dtype),
        ],
        in_specs=[any_space] * 3,
        out_specs=[any_space] * 5,
        scratch_shapes=[dma(size) for size in sizes],
        compiler_params=pltpu.CompilerParams(collective_id=1, has_side_effects=True),
        name="gather",
    )(tile, ids, lifted)


def split(wide, terms=3):
    out = []
    for _ in range(terms - 1):
        term = wide.astype(jnp.bfloat16).astype(jnp.float32)
        out.append(term)
        wide = wide - term
    return out + [wide]


def select_rows(one_hot, wide):
    return sum(jnp.dot(one_hot, term.astype(jnp.bfloat16), preferred_element_type=jnp.float32)
               for term in split(wide))


def as_one_hot(where_true):
    return jnp.where(where_true, 1.0, 0.0).astype(jnp.bfloat16)


def couple(far, coupling, parents, all_lifted, lifted, moved, own_locals):
    total, rank = own_locals.shape
    pairs = far.shape[1]
    for u in range(4):
        lifted[pl.ds(u, all_lifted.shape[0], stride=4), :] = pltpu.roll(all_lifted[...], (4 - u) % 4 * rank, 1)
    parent_row = lax.broadcasted_iota(jnp.int32, (total, 1), 0)
    moments = select_rows(as_one_hot(parent_row == parents[...]), lifted[:, :rank])
    lane = lax.broadcasted_iota(jnp.int32, (pairs, total), 1).astype(jnp.float32)
    sources = []
    for side in range(2):
        column = jnp.broadcast_to(far[side:side + 1, :].astype(jnp.float32), (8, pairs)).T[:, 0:1]
        sources.append(select_rows(as_one_hot(lane == column), moments))
    turned = sources[0].T
    pair_lane = lax.broadcasted_iota(jnp.int32, (rank, pairs), 1)
    to_first = jnp.zeros((rank, pairs), jnp.float32)
    for k in range(pairs):
        block = coupling[k]
        to_first = jnp.where(pair_lane == k, jnp.sum(block * sources[1][k:k + 1], axis=1, keepdims=True), to_first)
        moved[k:k + 1, :] = jnp.sum(block * turned[:, k:k + 1], axis=0, keepdims=True)
    own_locals[...] = (select_rows(as_one_hot(parent_row == far[0:1, :]), to_first.T)
                       + select_rows(as_one_hot(parent_row == far[1:2, :]), moved[...]))


def placement(row_ids, col_ids, place):
    per_device, slots = place.shape[0], row_ids.shape[2]
    n_row, n_col = col_ids.shape[0], row_ids.shape[0]
    row, col = lax.axis_index("row"), lax.axis_index("col")
    base = (row * n_col + col) * per_device
    lane = lax.broadcasted_iota(jnp.int32, (8, slots), 1)
    cluster = lax.broadcasted_iota(jnp.int32, (per_device, slots), 0) + base
    for ids, side, sources, mine, start in ((row_ids, 0, n_col, col, 0), (col_ids, 1, n_row, row, slots)):
        size = slots // sources
        owners = jnp.zeros((8, slots), jnp.int32)
        for src in range(sources):
            from_src = jnp.broadcast_to(ids[src, side:side + 1, :], (8, slots))
            shift = lax.rem((src - mine) * size + slots, slots)
            owners = jnp.where(lane // size == src, pltpu.roll(from_src, shift, 1), owners)
        place[:, start:start + slots] = as_one_hot(cluster == owners[0:1, :])


def near_kernel(per_device, pairs, live, row_tiles, col_tiles, far, coupling, parents, all_lifted, row_ids, col_ids,
                out_first, out_second, own_locals, place, row_wide, col_wide, lifted, moved, radius_sq, inv, cube):
    for narrow, wide in ((row_tiles, row_wide), (col_tiles, col_wide)):
        for src in range(narrow.shape[0] // (6 * per_device)):
            for i in range(8):
                if i < 6:
                    start = (src * 6 + i) * per_device
                    rows = narrow[start:start + per_device, :].astype(jnp.float32)
                else:
                    rows = jnp.full((per_device, narrow.shape[1]), 7.0 - i, jnp.float32)
                for half in range(2):
                    at = pl.ds(src * per_device * 8 + i, per_device, stride=8)
                    wide[half, at, :] = rows[:, half * 128:(half + 1) * 128]

    couple(far, coupling, parents, all_lifted, lifted, moved, own_locals)
    placement(row_ids, col_ids, place)
    row_span = per_device * row_ids.shape[0]
    row_base = lax.axis_index("row") * row_span
    out_first[...] = jnp.zeros_like(out_first)
    out_second[...] = jnp.zeros_like(out_second)
    panels = row_tiles.shape[1]
    count = live[0]
    eps_sq = REG_EPS * REG_EPS
    across = (((1,), (1,)), ((), ()))
    down = (((1,), (0,)), ((), ()))

    sub = lax.broadcasted_iota(jnp.int32, (8, panels), 0)
    ones = jnp.ones((1, panels), jnp.float32)

    def prepare(tile):
        products = [tile * tile[3 + i:4 + i, :] for i in range(3)]
        y_f = products[0][0:1] + products[1][1:2] + products[2][2:3]
        y_y = products[0][3:4] + products[1][4:5] + products[2][5:6]
        blocks = [tile]
        for product in products:
            high = product.astype(jnp.bfloat16).astype(jnp.float32)
            blocks += [high, product - high]
        blocks += split(tile * y_f)
        return jnp.concatenate(blocks, axis=0).astype(jnp.bfloat16), y_y

    def distances(ta, tb, xx, yy, u):
        x_high, x_mid, x_low = split(xx)
        y_high, y_mid, y_low = split(yy + eps_sq)
        left0 = jnp.where(sub == 0, x_high, jnp.where(sub == 1, x_mid, jnp.where(sub == 2, x_low, jnp.where(
            sub < 6, -2.0 * ta, ta))))
        right0 = jnp.where(sub < 3, ones, jnp.where(sub == 6, y_high, tb))
        left1 = jnp.where(sub < 2, ones, 0.0)
        right1 = jnp.where(sub == 0, y_mid, jnp.where(sub == 1, y_low, 0.0))
        left = jnp.concatenate([left0, left1], axis=0).T.astype(jnp.bfloat16)
        right = jnp.concatenate([right0, right1], axis=0).astype(jnp.bfloat16)
        radius_sq[u] = jnp.dot(left, right, preferred_element_type=jnp.float32)

    def combine(near_inv, near_cube, tile):
        x = tile[3:6]
        s = near_cube[0:3]
        value = near_inv[0:3] + eps_sq * s
        last = near_cube[56:64] + near_cube[64:72] + near_cube[72:80]
        dotted = jnp.sum(x * s, axis=0, keepdims=True) - last[6:7]
        value = value + (x * dotted + last[3:6])
        cross = [jnp.sum(x * (near_cube[8 + 16 * i:11 + 16 * i] + near_cube[16 + 16 * i:19 + 16 * i]), axis=0,
                         keepdims=True) for i in range(3)]
        return [(value[i:i + 1] - cross[i]) * STOKES_SCALE for i in range(3)]

    def fetch(wide, local):
        at = pl.ds(pl.multiple_of(local * 8, 8), 8)
        return jnp.concatenate([wide[0, at, :], wide[1, at, :]], axis=1)

    def begin(slot, u):
        b = pairs[1, slot]
        ta = fetch(row_wide, pairs[0, slot] - row_base)
        tb = fetch(col_wide, b // row_span * per_device + b % per_device)
        ra, xx = prepare(ta)
        rb, yy = prepare(tb)
        distances(ta, tb, xx, yy, u)
        return ta, tb, ra, rb

    def finish(slot, u, ta, tb, ra, rb):
        for chunk in range(panels // CHUNK):
            at = slice(chunk * CHUNK, (chunk + 1) * CHUNK)
            inv_dist = lax.rsqrt(radius_sq[u, at, :])
            inv[u, at, :] = inv_dist.astype(jnp.bfloat16)
            cube[u, at, :] = (inv_dist * inv_dist * inv_dist).astype(jnp.bfloat16)
        product = functools.partial(lax.dot_general, preferred_element_type=jnp.float32)
        to_first = combine(product(rb[0:16], inv[u], across), product(rb, cube[u], across), ta)
        to_second = combine(product(ra[0:16], inv[u], down), product(ra, cube[u], down), tb)
        within = slot < count
        keep_second = within & (pairs[0, slot] != pairs[1, slot])
        for i in range(3):
            at = slice(i * panels, (i + 1) * panels)
            out_first[pl.ds(slot, 1), at] = jnp.where(within, to_first[i], 0.0)
            out_second[pl.ds(slot, 1), at] = jnp.where(keep_second, to_second[i], 0.0)

    def group(step, carry):
        held = begin(step * GROUP, 0)
        for u in range(GROUP):
            ahead = begin(step * GROUP + u + 1, u + 1) if u + 1 < GROUP else None
            finish(step * GROUP + u, u, *held)
            held = ahead
        return carry

    lax.fori_loop(0, (count + GROUP - 1) // GROUP, group, 0)


def near(per_device, pairs, live, row_tiles, col_tiles, far, coupling, parents, all_lifted, row_ids, col_ids):
    slots, panels = pairs.shape[1], row_tiles.shape[1]
    rank, clusters = coupling.shape[1], parents.shape[1]
    smem = pl.BlockSpec(memory_space=pltpu.SMEM)
    vmem = pl.BlockSpec(memory_space=pltpu.VMEM)
    shape = jax.ShapeDtypeStruct
    return pl.pallas_call(
        functools.partial(near_kernel, per_device),
        out_shape=[shape((slots, 3 * panels), jnp.float32)] * 2 + [
            shape((clusters // 4, rank), jnp.float32), shape((per_device, 2 * slots), jnp.bfloat16)],
        in_specs=[smem, smem] + [vmem] * 8,
        out_specs=[vmem] * 4,
        scratch_shapes=[
            pltpu.VMEM((2, row_tiles.shape[0] // 6 * 8, 128), jnp.float32),
            pltpu.VMEM((2, col_tiles.shape[0] // 6 * 8, 128), jnp.float32),
            pltpu.VMEM((clusters, 4 * rank), jnp.float32),
            pltpu.VMEM((coupling.shape[0], rank), jnp.float32),
            pltpu.VMEM((GROUP, panels, panels), jnp.float32),
        ] + [pltpu.VMEM((GROUP, panels, panels), jnp.bfloat16)] * 2,
        compiler_params=pltpu.CompilerParams(vmem_limit_bytes=48 * 1024 * 1024),
        name="near",
    )(pairs, live, row_tiles, col_tiles, far, coupling, parents, all_lifted, row_ids, col_ids)


def exchange_kernel(n_row, n_col, parent, out_first, out_second, partial, place, transfer, basis, velocity,
                    got_first, got_second, total, f1, f2, acc, red, parts, coef, far_part, own_sem, s1, r1, s2, r2, s3, r3, sa, ra, sb, rb):
    row, col = lax.axis_index("row"), lax.axis_index("col")
    ca, cb = out_first.shape[0] // n_col, out_second.shape[0] // n_row
    piece = partial.shape[0] // n_col
    own = [
        pltpu.make_async_copy(part(out_first, col, ca), part(got_first, col, ca), own_sem.at[0]),
        pltpu.make_async_copy(part(out_second, row, cb), part(got_second, row, cb), own_sem.at[1]),
    ]
    for copy in own:
        copy.start()
    f1[pl.ds(col, 1)] = partial[pl.ds(pl.multiple_of(col * piece, piece), piece), :][None]
    greet(n_row, n_col, row, col)
    started = []

    def send(src, dst, sends, recvs, slot, mine, device):
        copy = pltpu.make_async_remote_copy(
            src_ref=src, dst_ref=dst, send_sem=sends.at[slot], recv_sem=recvs.at[mine],
            device_id=device, device_id_type=MESH)
        copy.start()
        started.append(copy)

    for k in range(1, n_col):
        peer = lax.rem(col + k, n_col)
        send(part(partial, peer, piece), f1.at[col], s1, r1, peer, col, (row, peer))
    for k in range(1, n_col):
        peer = lax.rem(col + k, n_col)
        send(part(out_first, peer, ca), part(got_first, col, ca), sa, ra, peer, col, (row, peer))
    for k in range(1, n_row):
        peer = lax.rem(row + k, n_row)
        send(part(out_second, peer, cb), part(got_second, row, cb), sb, rb, peer, row, (peer, col))

    for k in range(1, n_col):
        src = lax.rem(col + k, n_col)
        pltpu.make_async_copy(f1.at[src], f1.at[src], r1.at[src]).wait()
    acc[...] = jnp.sum(f1[...], axis=0)
    f2[pl.ds(row, 1)] = acc[...][None]
    for k in range(1, n_row):
        peer = lax.rem(row + k, n_row)
        send(acc, f2.at[row], s2, r2, peer, row, (peer, col))
    for k in range(1, n_row):
        src = lax.rem(row + k, n_row)
        pltpu.make_async_copy(f2.at[src], f2.at[src], r2.at[src]).wait()
    red[...] = jnp.sum(f2[...], axis=0)
    keep = pltpu.make_async_copy(red, part(total, col, piece), own_sem.at[2])
    keep.start()
    for k in range(1, n_col):
        peer = lax.rem(col + k, n_col)
        send(red, part(total, col, piece), s3, r3, peer, col, (row, peer))
    for k in range(1, n_col):
        src = lax.rem(col + k, n_col)
        pltpu.make_async_copy(red, part(total, src, piece), r3.at[src]).wait()
    keep.wait()

    per_device, rank = parts.shape
    base = (row * n_col + col) * per_device
    for c in range(per_device):
        parts[c:c + 1, :] = total[pl.ds(parent[base + c], 1), :]
    turned = parts[...].T
    for c in range(per_device):
        coef[c:c + 1, :] = jnp.sum(transfer[c] * turned[:, c:c + 1], axis=0, keepdims=True)
    turned = coef[...].T
    for c in range(per_device):
        far_part[c:c + 1, :] = jnp.sum(basis[c].astype(jnp.float32) * turned[:, c:c + 1], axis=0, keepdims=True)

    for k in range(1, n_col):
        src = lax.rem(col + k, n_col)
        view = part(got_first, src, ca)
        pltpu.make_async_copy(view, view, ra.at[src]).wait()
    for k in range(1, n_row):
        src = lax.rem(row + k, n_row)
        view = part(got_second, src, cb)
        pltpu.make_async_copy(view, view, rb.at[src]).wait()
    for copy in own:
        copy.wait()
    slots = got_first.shape[0]
    velocity[...] = (far_part[...] + select_rows(place[:, :slots], got_first[...])
                     + select_rows(place[:, slots:], got_second[...]))
    for copy in started:
        copy.wait_send()


def exchange(n_row, n_col, parent, out_first, out_second, partial, place, transfer, basis):
    smem = pl.BlockSpec(memory_space=pltpu.SMEM)
    vmem = pl.BlockSpec(memory_space=pltpu.VMEM)
    dma = pltpu.SemaphoreType.DMA
    piece, rank = partial.shape[0] // n_col, partial.shape[1]
    per_device, width = place.shape[0], out_first.shape[1]
    sizes = [3, n_col, n_col, n_row, n_row, n_col, n_col, n_col, n_col, n_row, n_row]
    buffers = [out_first.shape, out_second.shape, partial.shape, (n_col, piece, rank), (n_row, piece, rank),
               (piece, rank), (piece, rank), (per_device, rank), (per_device, rank), (per_device, width)]
    return pl.pallas_call(
        functools.partial(exchange_kernel, n_row, n_col),
        out_shape=jax.ShapeDtypeStruct((per_device, width), jnp.float32),
        in_specs=[smem] + [vmem] * 6,
        out_specs=vmem,
        scratch_shapes=[pltpu.VMEM(size, jnp.float32) for size in buffers] + [dma((size,)) for size in sizes],
        compiler_params=pltpu.CompilerParams(
            collective_id=2, has_side_effects=True, vmem_limit_bytes=32 * 1024 * 1024),
        name="exchange",
    )(parent, out_first, out_second, partial, place, transfer, basis)


def shards(density, coords, basis, transfer, parent, near_pairs, near_count, far_pairs, coupling):
    highest = lax.Precision.HIGHEST
    per_device, _, panels = density.shape
    n_row, n_col = lax.axis_size("row"), lax.axis_size("col")
    tile = jnp.concatenate([density, coords], axis=1).transpose(1, 0, 2).reshape(6 * per_device, panels)
    flattened = density.reshape(per_device, 3 * panels)
    moments = jnp.einsum("crk,ck->cr", basis, flattened, preferred_element_type=jnp.float32)
    lifted = jnp.einsum("crs,cs->cr", transfer, moments, precision=highest)
    row_tiles, col_tiles, row_ids, col_ids, all_lifted = gather(
        n_row, n_col, tile, near_pairs, lifted.reshape(-1, 128))
    out_first, out_second, own_locals, place = near(
        per_device, near_pairs, near_count, row_tiles, col_tiles, far_pairs, coupling, parent.reshape(1, -1),
        all_lifted, row_ids, col_ids)
    velocity = exchange(n_row, n_col, parent, out_first, out_second, own_locals, place, transfer, basis)
    return velocity.reshape(per_device, 3, panels)


def solution(mesh):
    placed = (
        P(("row", "col"), None, None),
        P(("row", "col"), None, None),
        P(("row", "col"), None, None),
        P(("row", "col"), None, None),
        P(),
        P(None, ("row", "col")),
        P(("row", "col")),
        P(None, ("row", "col")),
        P(("row", "col"), None, None),
    )
    return jax.shard_map(
        shards, mesh=mesh, in_specs=placed, out_specs=P(("row", "col"), None, None), check_vma=False
    )
```

profile of v0, /device:TPU:0, one launch (start us, length us, event | category | flops | bytes accessed | tf_op | source)
XLA Modules:
  0.0 81.6 jit_solution(13841947656384943643)
XLA Ops:
  0.8 0.8 %copy.12 = bf16[32,3,256]{2,1,0:T(4,128)(2,1)S(1)} copy(bf16[32,3,256]{2,0,1:T(8,128)(2,1)} %param.9) | data formatting | bytes 98304 | tf_op args[0]
  1.6 0.1 reshape.25
  1.7 1.9 %convolution_bitcast_fusion = f32[32,32,1]{1,2,0:T(1,128)S(1)} fusion(bf16[32,32,768]{2,1,0:T(8,128)(2,1)} %basis.1, bf16[32,768,1]{1,2,0:T(2,128)(2,1)S(1)} %reshape.25), kind=kOutput, calls=%fused_computation | convolution fusion | flops 1572864 | bytes 1626112 | tf_op jit(solution)/shard_map/crk,ck->cr/dot_general | solution.py:438
  3.6 0.0 copy-done
  3.6 0.0 copy-start.9
  3.6 0.9 %fusion = f32[32,1,32]{2,1,0:T(1,128)S(1)} fusion(f32[32,32,1]{1,2,0:T(1,128)S(1)} %convolution_bitcast_fusion, f32[32,32,32]{2,1,0:T(8,128)S(1)} %copy-done), kind=kOutput, calls=%fused_computation.3 | convolution fusion | flops 393216 | bytes 139264 | tf_op jit(solution)/shard_map/crs,cs->cr/dot_general | solution.py:439
  4.5 0.7 reshape.17.lifted
  5.2 0.0 copy-done.11
  5.2 0.0 copy-done.12
  5.2 0.7 pad_maximum_fusion
  5.9 0.0 copy-done.10
  5.9 0.9 %copy.13.coupling = f32[64,32,32]{2,1,0:T(8,128)S(1)} copy(f32[64,32,32]{0,2,1:T(8,128)S(1)} %copy-done.10) | data formatting | bytes 524288 | tf_op args[8]
  6.8 0.0 copy-start.1
  6.8 22.0 %gather.1 = (bf16[1536,256]{1,0:T(8,128)(2,1)}, bf16[768,256]{1,0:T(8,128)(2,1)}, s32[8,2,128]{2,1,0:T(2,128)}, s32[4,2,128]{2,1,0:T(2,128)}, f32[256,128]{1,0:T(8,128)}) custom-call(bf16[192,256]{1,0:T(8,128)(2,1)} %bitcast.22, s32[2,128]{1,0:T(2,128)} %pairs.1, f32[8,128]{1,0:T(8,128)} %reshape.17.lifted), custom_call_target="tpu_custom_call" | custom-call | tf_op jit(solution)/shard_map/gather/pallas_call | solution.py:127
  28.8 0.0 copy-done.5
  28.8 0.0 copy-done.8
  28.9 1.1 %copy-done.2 = bf16[1536,256]{1,0:T(8,128)(2,1)S(1)} copy-done((bf16[1536,256]{1,0:T(8,128)(2,1)S(1)}, bf16[1536,256]{1,0:T(8,128)(2,1)}, u32[]{:S(2)}) %copy-start.2) | copy-done | bytes 786456
  30.0 1.0 %copy-done.3 = bf16[768,256]{1,0:T(8,128)(2,1)S(1)} copy-done((bf16[768,256]{1,0:T(8,128)(2,1)S(1)}, bf16[768,256]{1,0:T(8,128)(2,1)}, u32[]{:S(2)}) %copy-start.3) | copy-done | bytes 393240
  31.0 0.9 %copy-done.4 = f32[256,128]{1,0:T(8,128)S(1)} copy-done((f32[256,128]{1,0:T(8,128)S(1)}, f32[256,128]{1,0:T(8,128)}, u32[]{:S(2)}) %copy-start.4) | copy-done | bytes 131096
  31.9 0.7 copy-done.6
  32.6 0.7 copy-done.7
  33.3 11.9 %near.1 = (f32[128,768]{1,0:T(8,128)S(1)}, f32[128,768]{1,0:T(8,128)S(1)}, f32[256,32]{1,0:T(8,128)S(1)}, bf16[32,256]{1,0:T(8,128)(2,1)S(1)}) custom-call(s32[2,128]{1,0:T(2,128)S(1)} %copy-done.8, s32[1]{0:T(128)S(6)} %copy.22.live, bf16[1536,256]{1,0:T(8,128)(2,1)S(1)} %copy-done.2, bf16[768,256]{1,0:T(8,128)(2,1)S(1)} %copy-done.3, ...), custom_call_target="tpu_custom_call" | custom-call | tf_op jit(solution)/shard_map/near/pallas_call | solution.py:311
  45.2 35.8 %exchange.1 = f32[32,768]{1,0:T(8,128)S(1)} custom-call(s32[1024]{0:T(1024)S(1)} %copy-done.5, f32[128,768]{1,0:T(8,128)S(1)} %get-tuple-element.19.out_first, f32[128,768]{1,0:T(8,128)S(1)} %get-tuple-element.20.out_second, f32[256,32]{1,0:T(8,128)S(1)} %get-tuple-element.21.partial, bf16[32,256]{1,0:T(8,128)(2,1)S(1)} %get-tuple-element.22.place, ...), custom_call_target="tpu_custom_call" | custom-call | tf_op jit(solution)/shard_map/exchange/pallas_call | solution.py:420
  81.0 0.6 copy.21
  (13 shorter events, 0.0 us)
Async XLA Ops:
  0.0 3.6 %copy-start = (f32[32,32,32]{2,1,0:T(8,128)S(1)}, f32[32,32,32]{2,1,0:T(8,128)}, u32[]{:S(2)}) copy-start(f32[32,32,32]{2,1,0:T(8,128)} %transfer.1) | copy-start | bytes 393220
  0.0 5.2 %copy-start.11 = (bf16[32,3,256]{2,0,1:T(8,128)(2,1)S(1)}, bf16[32,3,256]{2,0,1:T(8,128)(2,1)}, u32[]{:S(2)}) copy-start(bf16[32,3,256]{2,0,1:T(8,128)(2,1)} %param.9) | copy-start | bytes 147460
  0.0 5.9 %copy-start.10 = (f32[64,32,32]{0,2,1:T(8,128)S(1)}, f32[64,32,32]{0,2,1:T(8,128)}, u32[]{:S(2)}) copy-start(f32[64,32,32]{0,2,1:T(8,128)} %param.17) | copy-start | bytes 786436
  0.0 5.2 %copy-start.12 = (bf16[32,3,256]{2,0,1:T(8,128)(2,1)S(1)}, bf16[32,3,256]{2,0,1:T(8,128)(2,1)}, u32[]{:S(2)}) copy-start(bf16[32,3,256]{2,0,1:T(8,128)(2,1)} %param.10) | copy-start | bytes 147460
  3.6 25.2 %copy-start.5 = (s32[1024]{0:T(1024)S(1)}, s32[1024]{0:T(1024)}, u32[]{:S(2)}) copy-start(s32[1024]{0:T(1024)} %parent.1) | copy-start | bytes 12292
  3.6 25.3 %copy-start.8 = (s32[2,128]{1,0:T(2,128)S(1)}, s32[2,128]{1,0:T(2,128)}, u32[]{:S(2)}) copy-start(s32[2,128]{1,0:T(2,128)} %pairs.1) | copy-start | bytes 3076
  3.6 25.3 %copy-start.9 = (s32[2,64]{1,0:T(2,128)S(1)}, s32[2,64]{1,0:T(2,128)}, u32[]{:S(2)}) copy-start(s32[2,64]{1,0:T(2,128)} %far.1) | copy-start | bytes 1540
  6.8 38.3 %copy-start.1 = (bf16[32,32,768]{2,1,0:T(8,128)(2,1)S(1)}, bf16[32,32,768]{2,1,0:T(8,128)(2,1)}, u32[]{:S(2)}) copy-start(bf16[32,32,768]{2,1,0:T(8,128)(2,1)} %basis.1) | copy-start | bytes 4718596
  28.8 1.1 %copy-start.2 = (bf16[1536,256]{1,0:T(8,128)(2,1)S(1)}, bf16[1536,256]{1,0:T(8,128)(2,1)}, u32[]{:S(2)}) copy-start(bf16[1536,256]{1,0:T(8,128)(2,1)} %get-tuple-element.14.row_tiles) | copy-start | bytes 2359300
  30.0 1.0 %copy-start.3 = (bf16[768,256]{1,0:T(8,128)(2,1)S(1)}, bf16[768,256]{1,0:T(8,128)(2,1)}, u32[]{:S(2)}) copy-start(bf16[768,256]{1,0:T(8,128)(2,1)} %get-tuple-element.15.col_tiles) | copy-start | bytes 1179652
  31.0 0.9 %copy-start.4 = (f32[256,128]{1,0:T(8,128)S(1)}, f32[256,128]{1,0:T(8,128)}, u32[]{:S(2)}) copy-start(f32[256,128]{1,0:T(8,128)} %get-tuple-element.16.all_lifted) | copy-start | bytes 393220
  31.9 0.7 copy-start.6
  32.6 0.7 copy-start.7
where the time goes:
time: 82 us; the launch traced here: 81.6 us
  Pallas kernels  69.7 us (85%)
  local copies, waits for them, and re-layouts  7.59 us (9%)
  matrix products  2.84 us (3%)
  between operations  0.85 us (1%)
    pallas_call x1, Pallas kernels, exchange(): pl.pallas_call(functools.partial(exchange_kernel, n_row, n_col), out_shap...  35.8 us
    pallas_call x1, Pallas kernels, gather(): pl.pallas_call(functools.partial(gather_kernel, n_row, n_col, n_z), out_s...  22 us
    pallas_call x1, Pallas kernels, near(): pl.pallas_call(functools.partial(near_kernel, per_device), out_shape=[sha...  11.9 us
    unnamed x28, local copies, waits for them, and re-layouts  6.22 us
    dot_general x1, matrix products, shards(): jnp.einsum('crk,ck->cr', basis, flattened, preferred_element_type=jnp.flo...  1.91 us

commit v1 on v0

--- a/solution.py
+++ b/solution.py
@@ -28,8 +28,28 @@
     return ref.at[pl.ds(pl.multiple_of(index * size, size), size)]
 
 
-def gather_kernel(n_row, n_col, n_z, tile, ids, lifted, row_tiles, col_tiles, row_ids, col_ids, all_lifted,
-                  own_sem, st, rt, sct, rct, si, ri, sci, rci, sl, rl, scl, rcl):
+def lift(tile, basis, transfer, lifted):
+    per_device, rank, width = basis.shape
+    panels = width // 3
+    source = tile[...].astype(jnp.float32)
+    lane = lax.broadcasted_iota(jnp.int32, (rank, per_device), 1)
+    turned = jnp.zeros((rank, per_device), jnp.float32)
+    for c in range(per_device):
+        total = sum(basis[c, :, i * panels:(i + 1) * panels].astype(jnp.float32)
+                    * source[i * per_device + c:i * per_device + c + 1] for i in range(3))
+        turned = jnp.where(lane == c, jnp.sum(total, axis=1, keepdims=True), turned)
+    moments = turned.T
+    turned = jnp.zeros((rank, per_device), jnp.float32)
+    for c in range(per_device):
+        total = jnp.sum(transfer[c] * moments[c:c + 1], axis=1, keepdims=True)
+        turned = jnp.where(lane == c, total, turned)
+    value = turned.T
+    group = per_device // 4
+    lifted[...] = jnp.concatenate([value[u * group:(u + 1) * group] for u in range(4)], axis=1)
+
+
+def gather_kernel(n_row, n_col, n_z, tile, ids, basis, transfer, row_tiles, col_tiles, row_ids, col_ids, all_lifted,
+                  lifted, own_sem, st, rt, sct, rct, si, ri, sci, rci, sl, rl, scl, rcl):
     row, col = lax.axis_index("row"), lax.axis_index("col")
     n_y = n_col // n_z
     z, y = col // n_y, lax.rem(col, n_y)
@@ -42,7 +62,7 @@
         pltpu.make_async_copy(ids, col_ids.at[row], own_sem.at[3]),
         pltpu.make_async_copy(lifted, part(all_lifted, row * n_col + col, lift_rows), own_sem.at[4]),
     ]
-    for copy in own:
+    for copy in own[:4]:
         copy.start()
     greet(n_row, n_col, row, col)
 
@@ -62,11 +82,6 @@
         copy.start()
         started.append(copy)
 
-    for k in range(1, n_col):
-        peer = lax.rem(col + k, n_col)
-        go(pltpu.make_async_remote_copy(
-            src_ref=lifted, dst_ref=part(all_lifted, row * n_col + col, lift_rows),
-            send_sem=sl.at[peer], recv_sem=rl.at[col], device_id=(row, peer), device_id_type=MESH))
     for k in range(1, n_z):
         peer = lax.rem(z + k, n_z) * n_y + y
         go(to_col(tile, row_tiles, col, rows, st, rt, k, peer))
@@ -83,6 +98,13 @@
             src_ref=ids, dst_ref=row_ids.at[col], send_sem=si.at[peer], recv_sem=ri.at[col],
             device_id=(row, peer), device_id_type=MESH))
 
+    lift(tile, basis, transfer, lifted)
+    own[4].start()
+    for k in range(1, n_col):
+        peer = lax.rem(col + k, n_col)
+        go(pltpu.make_async_remote_copy(
+            src_ref=lifted, dst_ref=part(all_lifted, row * n_col + col, lift_rows),
+            send_sem=sl.at[peer], recv_sem=rl.at[col], device_id=(row, peer), device_id_type=MESH))
     own[4].wait()
     for k in range(1, n_col):
         src = lax.rem(col + k, n_col)
@@ -117,13 +139,14 @@
         copy.wait_send()
 
 
-def gather(n_row, n_col, tile, ids, lifted):
+def gather(n_row, n_col, tile, ids, basis, transfer):
     n_z = 4 if n_col % 4 == 0 else 1
-    any_space = pl.BlockSpec(memory_space=pl.ANY)
+    vmem = pl.BlockSpec(memory_space=pltpu.VMEM)
     dma = pltpu.SemaphoreType.DMA
     sizes = [(5,), (n_z * (n_col // n_z + 1) + n_col,), (n_col,), (n_row,), (n_row,), (n_col,), (n_col,),
              (n_row,), (n_row,), (n_col,), (n_col,), (n_row,), (n_row,)]
     shape = jax.ShapeDtypeStruct
+    lift_shape = (basis.shape[0] // 4, 4 * basis.shape[1])
     return pl.pallas_call(
         functools.partial(gather_kernel, n_row, n_col, n_z),
         out_shape=[
@@ -131,14 +154,15 @@
             shape((n_row * tile.shape[0], tile.shape[1]), tile.dtype),
             shape((n_col,) + ids.shape, ids.dtype),
             shape((n_row,) + ids.shape, ids.dtype),
-            shape((n_row * n_col * lifted.shape[0], lifted.shape[1]), lifted.dtype),
+            shape((n_row * n_col * lift_shape[0], lift_shape[1]), jnp.float32),
         ],
-        in_specs=[any_space] * 3,
-        out_specs=[any_space] * 5,
-        scratch_shapes=[dma(size) for size in sizes],
-        compiler_params=pltpu.CompilerParams(collective_id=1, has_side_effects=True),
+        in_specs=[vmem] * 4,
+        out_specs=[vmem] * 5,
+        scratch_shapes=[pltpu.VMEM(lift_shape, jnp.float32)] + [dma(size) for size in sizes],
+        compiler_params=pltpu.CompilerParams(
+            collective_id=1, has_side_effects=True, vmem_limit_bytes=32 * 1024 * 1024),
         name="gather",
-    )(tile, ids, lifted)
+    )(tile, ids, basis, transfer)
 
 
 def split(wide, terms=3):
@@ -163,9 +187,11 @@
     total, rank = own_locals.shape
     pairs = far.shape[1]
     for u in range(4):
-        lifted[pl.ds(u, all_lifted.shape[0], stride=4), :] = pltpu.roll(all_lifted[...], (4 - u) % 4 * rank, 1)
+        turned = pltpu.roll(all_lifted[...], (4 - u) % 4 * rank, 1)
+        lifted[:, u] = turned.reshape(lifted.shape[0], lifted.shape[2], 4 * rank)
+    clusters = parents.shape[1]
     parent_row = lax.broadcasted_iota(jnp.int32, (total, 1), 0)
-    moments = select_rows(as_one_hot(parent_row == parents[...]), lifted[:, :rank])
+    moments = select_rows(as_one_hot(parent_row == parents[...]), lifted[...].reshape(clusters, 4 * rank)[:, :rank])
     lane = lax.broadcasted_iota(jnp.int32, (pairs, total), 1).astype(jnp.float32)
     sources = []
     for side in range(2):
@@ -200,7 +226,7 @@
 
 
 def near_kernel(per_device, pairs, live, row_tiles, col_tiles, far, coupling, parents, all_lifted, row_ids, col_ids,
-                out_first, out_second, own_locals, place, row_wide, col_wide, lifted, moved, radius_sq, inv, cube):
+                sent_first, sent_second, own_locals, place, out_first, out_second, row_wide, col_wide, lifted, moved, radius_sq, inv, cube):
     for narrow, wide in ((row_tiles, row_wide), (col_tiles, col_wide)):
         for src in range(narrow.shape[0] // (6 * per_device)):
             for i in range(8):
@@ -300,6 +326,10 @@
         return carry
 
     lax.fori_loop(0, (count + GROUP - 1) // GROUP, group, 0)
+    for out, sent in ((out_first, sent_first), (out_second, sent_second)):
+        size = sent.shape[1]
+        for k in range(sent.shape[0]):
+            sent[k] = out[k * size:(k + 1) * size, :].astype(jnp.bfloat16)
 
 
 def near(per_device, pairs, live, row_tiles, col_tiles, far, coupling, parents, all_lifted, row_ids, col_ids):
@@ -310,14 +340,14 @@
     shape = jax.ShapeDtypeStruct
     return pl.pallas_call(
         functools.partial(near_kernel, per_device),
-        out_shape=[shape((slots, 3 * panels), jnp.float32)] * 2 + [
+        out_shape=[shape((n, slots // n, 3 * panels), jnp.bfloat16) for n in (row_ids.shape[0], col_ids.shape[0])] + [
             shape((clusters // 4, rank), jnp.float32), shape((per_device, 2 * slots), jnp.bfloat16)],
         in_specs=[smem, smem] + [vmem] * 8,
         out_specs=[vmem] * 4,
-        scratch_shapes=[
+        scratch_shapes=[pltpu.VMEM((slots, 3 * panels), jnp.float32)] * 2 + [
             pltpu.VMEM((2, row_tiles.shape[0] // 6 * 8, 128), jnp.float32),
             pltpu.VMEM((2, col_tiles.shape[0] // 6 * 8, 128), jnp.float32),
-            pltpu.VMEM((clusters, 4 * rank), jnp.float32),
+            pltpu.VMEM((clusters // per_device, 4, per_device // 4, 4 * rank), jnp.float32),
             pltpu.VMEM((coupling.shape[0], rank), jnp.float32),
             pltpu.VMEM((GROUP, panels, panels), jnp.float32),
         ] + [pltpu.VMEM((GROUP, panels, panels), jnp.bfloat16)] * 2,
@@ -329,11 +359,10 @@
 def exchange_kernel(n_row, n_col, parent, out_first, out_second, partial, place, transfer, basis, velocity,
                     got_first, got_second, total, f1, f2, acc, red, parts, coef, far_part, own_sem, s1, r1, s2, r2, s3, r3, sa, ra, sb, rb):
     row, col = lax.axis_index("row"), lax.axis_index("col")
-    ca, cb = out_first.shape[0] // n_col, out_second.shape[0] // n_row
     piece = partial.shape[0] // n_col
     own = [
-        pltpu.make_async_copy(part(out_first, col, ca), part(got_first, col, ca), own_sem.at[0]),
-        pltpu.make_async_copy(part(out_second, row, cb), part(got_second, row, cb), own_sem.at[1]),
+        pltpu.make_async_copy(out_first.at[col], got_first.at[col], own_sem.at[0]),
+        pltpu.make_async_copy(out_second.at[row], got_second.at[row], own_sem.at[1]),
     ]
     for copy in own:
         copy.start()
@@ -353,10 +382,10 @@
         send(part(partial, peer, piece), f1.at[col], s1, r1, peer, col, (row, peer))
     for k in range(1, n_col):
         peer = lax.rem(col + k, n_col)
-        send(part(out_first, peer, ca), part(got_first, col, ca), sa, ra, peer, col, (row, peer))
+        send(out_first.at[peer], got_first.at[col], sa, ra, peer, col, (row, peer))
     for k in range(1, n_row):
         peer = lax.rem(row + k, n_row)
-        send(part(out_second, peer, cb), part(got_second, row, cb), sb, rb, peer, row, (peer, col))
+        send(out_second.at[peer], got_second.at[row], sb, rb, peer, row, (peer, col))
 
     for k in range(1, n_col):
         src = lax.rem(col + k, n_col)
@@ -393,17 +422,20 @@
 
     for k in range(1, n_col):
         src = lax.rem(col + k, n_col)
-        view = part(got_first, src, ca)
+        view = got_first.at[src]
         pltpu.make_async_copy(view, view, ra.at[src]).wait()
     for k in range(1, n_row):
         src = lax.rem(row + k, n_row)
-        view = part(got_second, src, cb)
+        view = got_second.at[src]
         pltpu.make_async_copy(view, view, rb.at[src]).wait()
     for copy in own:
         copy.wait()
-    slots = got_first.shape[0]
-    velocity[...] = (far_part[...] + select_rows(place[:, :slots], got_first[...])
-                     + select_rows(place[:, slots:], got_second[...]))
+    slots = place.shape[1] // 2
+    value = far_part[...]
+    for got, start in ((got_first, 0), (got_second, slots)):
+        rows = got[...].astype(jnp.float32).reshape(slots, got.shape[2]).astype(jnp.bfloat16)
+        value = value + jnp.dot(place[:, start:start + slots], rows, preferred_element_type=jnp.float32)
+    velocity[...] = value
     for copy in started:
         copy.wait_send()
 
@@ -413,16 +445,17 @@
     vmem = pl.BlockSpec(memory_space=pltpu.VMEM)
     dma = pltpu.SemaphoreType.DMA
     piece, rank = partial.shape[0] // n_col, partial.shape[1]
-    per_device, width = place.shape[0], out_first.shape[1]
+    per_device, width = place.shape[0], out_first.shape[2]
     sizes = [3, n_col, n_col, n_row, n_row, n_col, n_col, n_col, n_col, n_row, n_row]
-    buffers = [out_first.shape, out_second.shape, partial.shape, (n_col, piece, rank), (n_row, piece, rank),
+    buffers = [partial.shape, (n_col, piece, rank), (n_row, piece, rank),
                (piece, rank), (piece, rank), (per_device, rank), (per_device, rank), (per_device, width)]
     return pl.pallas_call(
         functools.partial(exchange_kernel, n_row, n_col),
         out_shape=jax.ShapeDtypeStruct((per_device, width), jnp.float32),
         in_specs=[smem] + [vmem] * 6,
         out_specs=vmem,
-        scratch_shapes=[pltpu.VMEM(size, jnp.float32) for size in buffers] + [dma((size,)) for size in sizes],
+        scratch_shapes=[pltpu.VMEM(out_first.shape, jnp.bfloat16), pltpu.VMEM(out_second.shape, jnp.bfloat16)] + [
+            pltpu.VMEM(size, jnp.float32) for size in buffers] + [dma((size,)) for size in sizes],
         compiler_params=pltpu.CompilerParams(
             collective_id=2, has_side_effects=True, vmem_limit_bytes=32 * 1024 * 1024),
         name="exchange",
@@ -430,15 +463,11 @@
 
 
 def shards(density, coords, basis, transfer, parent, near_pairs, near_count, far_pairs, coupling):
-    highest = lax.Precision.HIGHEST
     per_device, _, panels = density.shape
     n_row, n_col = lax.axis_size("row"), lax.axis_size("col")
     tile = jnp.concatenate([density, coords], axis=1).transpose(1, 0, 2).reshape(6 * per_device, panels)
-    flattened = density.reshape(per_device, 3 * panels)
-    moments = jnp.einsum("crk,ck->cr", basis, flattened, preferred_element_type=jnp.float32)
-    lifted = jnp.einsum("crs,cs->cr", transfer, moments, precision=highest)
     row_tiles, col_tiles, row_ids, col_ids, all_lifted = gather(
-        n_row, n_col, tile, near_pairs, lifted.reshape(-1, 128))
+        n_row, n_col, tile, near_pairs, basis, transfer)
     out_first, out_second, own_locals, place = near(
         per_device, near_pairs, near_count, row_tiles, col_tiles, far_pairs, coupling, parent.reshape(1, -1),
         all_lifted, row_ids, col_ids)

time: 82 us -> 73.9 us (0.901)
  local copies, waits for them, and re-layouts: 7.59 us -> 3.69 us
  matrix products: 2.84 us -> 0 us
  Pallas kernels: 69.7 us -> 67.8 us
    unnamed x28 -> x13, local copies, waits for them, and re-layouts: 6.22 us -> 3.04 us
    pallas_call x1, Pallas kernels: 22 us -> 25 us  [gather(): pl.pallas_call(functools.partial(gather_kernel, n_row, n_col, n_z), out_s...]
    dot_general x2 -> x0, matrix products: 2.84 us -> none  [the longest x1 1.91 us: shards(): jnp.einsum('crk,ck->cr', basis, flattened, preferred_element_type=jnp.flo...]
    pallas_call x1, Pallas kernels: 11.9 us -> 9.25 us  [near(): pl.pallas_call(functools.partial(near_kernel, per_device), out_shape=[sha...]
    pallas_call x1, Pallas kernels: 35.8 us -> 33.5 us  [exchange(): pl.pallas_call(functools.partial(exchange_kernel, n_row, n_col), out_shap...]
where the time goes in v1:
time: 73.9 us; the launch traced here: 73.2 us
  Pallas kernels  67.8 us (92%)
  local copies, waits for them, and re-layouts  3.69 us (5%)
  between operations  0.88 us (1%)
  other arithmetic  0.83 us (1%)
    pallas_call x1, Pallas kernels, exchange(): pl.pallas_call(functools.partial(exchange_kernel, n_row, n_col), out_shap...  33.5 us
    pallas_call x1, Pallas kernels, gather(): pl.pallas_call(functools.partial(gather_kernel, n_row, n_col, n_z), out_s...  25 us
    pallas_call x1, Pallas kernels, near(): pl.pallas_call(functools.partial(near_kernel, per_device), out_shape=[sha...  9.25 us
    unnamed x13, local copies, waits for them, and re-layouts  3.04 us

profile of v1, /device:TPU:0, one launch (start us, length us, event | category | flops | bytes accessed | tf_op | source)
XLA Modules:
  0.0 73.2 jit_solution(1175641119193004578)
XLA Ops:
  0.0 0.0 copy-start.4
  0.0 0.0 copy-start
  0.8 0.8 %pad_maximum_fusion = bf16[32,6,256]{2,0,1:T(8,128)(2,1)S(1)} fusion(bf16[32,3,256]{2,0,1:T(8,128)(2,1)} %param.10, bf16[32,3,256]{2,0,1:T(8,128)(2,1)} %param.9), kind=kLoop, calls=%fused_computation.1 | loop fusion | flops 49152 | bytes 196608 | tf_op jit(solution)/shard_map/concatenate | solution.py:468
  1.6 0.0 copy-start.3
  1.6 0.0 copy-start.5
  1.6 2.0 %copy.12.coupling = f32[64,32,32]{2,1,0:T(8,128)S(1)} copy(f32[64,32,32]{0,2,1:T(8,128)} %param.17) | data formatting | bytes 524288 | tf_op args[8]
  3.6 0.0 copy-done.4
  3.6 0.0 copy-done
  3.6 0.0 copy-start.1
  3.7 1.0 %copy-done.1 = f32[32,32,32]{2,1,0:T(8,128)S(1)} copy-done((f32[32,32,32]{2,1,0:T(8,128)S(1)}, f32[32,32,32]{2,1,0:T(8,128)}, u32[]{:S(2)}) %copy-start.1) | copy-done | bytes 131096
  4.7 25.0 %gather.1 = (bf16[1536,256]{1,0:T(8,128)(2,1)S(1)}, bf16[768,256]{1,0:T(8,128)(2,1)S(1)}, s32[8,2,128]{2,1,0:T(2,128)S(1)}, s32[4,2,128]{2,1,0:T(2,128)S(1)}, f32[256,128]{1,0:T(8,128)S(1)}) custom-call(bf16[192,256]{1,0:T(8,128)(2,1)S(1)} %bitcast.8, s32[2,128]{1,0:T(2,128)S(1)} %copy-done.4, bf16[32,32,768]{2,1,0:T(8,128)(2,1)S(1)} %copy-done, ...), custom_call_target="tpu_custom_call" | custom-call | tf_op jit(solution)/shard_map/gather/pallas_call | solution.py:150
  29.7 0.0 copy-start.2
  29.7 0.0 copy-done.3
  29.7 0.0 copy-done.5
  29.8 9.2 %near.1 = (bf16[8,16,768]{2,1,0:T(8,128)(2,1)S(1)}, bf16[4,32,768]{2,1,0:T(8,128)(2,1)S(1)}, f32[256,32]{1,0:T(8,128)S(1)}, bf16[32,256]{1,0:T(8,128)(2,1)S(1)}) custom-call(s32[2,128]{1,0:T(2,128)S(1)} %copy-done.4, s32[1]{0:T(128)S(6)} %copy.17.live, bf16[1536,256]{1,0:T(8,128)(2,1)S(1)} %get-tuple-element.14.row_tiles, ...), custom_call_target="tpu_custom_call" | custom-call | tf_op jit(solution)/shard_map/near/pallas_call | solution.py:341
  39.0 0.0 copy-done.2
  39.0 33.5 %exchange.1 = f32[32,768]{1,0:T(8,128)S(1)} custom-call(s32[1024]{0:T(1024)S(1)} %copy-done.3, bf16[8,16,768]{2,1,0:T(8,128)(2,1)S(1)} %get-tuple-element.19.out_first, bf16[4,32,768]{2,1,0:T(8,128)(2,1)S(1)} %get-tuple-element.20.out_second, f32[256,32]{1,0:T(8,128)S(1)} %get-tuple-element.21.partial, bf16[32,256]{1,0:T(8,128)(2,1)S(1)} %get-tuple-element.22.place, ...), custom_call_target="tpu_custom_call" | custom-call | tf_op jit(solution)/shard_map/exchange/pallas_call | solution.py:452
  72.5 0.6 copy.16
Async XLA Ops:
  0.0 3.6 %copy-start.4 = (s32[2,128]{1,0:T(2,128)S(1)}, s32[2,128]{1,0:T(2,128)}, u32[]{:S(2)}) copy-start(s32[2,128]{1,0:T(2,128)} %pairs.1) | copy-start | bytes 3076
  0.0 3.6 %copy-start = (bf16[32,32,768]{2,1,0:T(8,128)(2,1)S(1)}, bf16[32,32,768]{2,1,0:T(8,128)(2,1)}, u32[]{:S(2)}) copy-start(bf16[32,32,768]{2,1,0:T(8,128)(2,1)} %basis.3) | copy-start | bytes 4718596
  1.6 28.1 %copy-start.3 = (s32[1024]{0:T(1024)S(1)}, s32[1024]{0:T(1024)}, u32[]{:S(2)}) copy-start(s32[1024]{0:T(1024)} %parent.1) | copy-start | bytes 12292
  1.6 28.1 %copy-start.5 = (s32[2,64]{1,0:T(2,128)S(1)}, s32[2,64]{1,0:T(2,128)}, u32[]{:S(2)}) copy-start(s32[2,64]{1,0:T(2,128)} %far.1) | copy-start | bytes 1540
  3.6 1.0 %copy-start.1 = (f32[32,32,32]{2,1,0:T(8,128)S(1)}, f32[32,32,32]{2,1,0:T(8,128)}, u32[]{:S(2)}) copy-start(f32[32,32,32]{2,1,0:T(8,128)} %transfer.3) | copy-start | bytes 393220
  29.7 9.3 %copy-start.2 = (f32[32,32,32]{2,1,0:T(8,128)S(1)}, f32[32,32,32]{2,1,0:T(8,128)}, u32[]{:S(2)}) copy-start(f32[32,32,32]{2,1,0:T(8,128)} %transfer.3) | copy-start | bytes 393220
